TPU v7x, 32 devices: a whole 2x2x4 slice. The times are simulated.
32 devices in a mesh: rep: 2 (over x), node: 4 (over y, core), tp: 4 (over z).
Axes of the slice: x: 2, y: 2, z: 4, core: 2. Of those that a mesh axis runs over, the one named last changes fastest.
Arguments:
- queries: bfloat16 [256, 6144], P(('rep', 'node'), 'tp'), parts along dimension 0, may hold values from -130 to 130
- cache_keys: bfloat16 [256, 8, 384, 128], P(('rep', 'node'), 'tp'), parts along dimension 0, may hold values from -6 to 6
- cache_values: bfloat16 [256, 8, 384, 128], P(('rep', 'node'), 'tp'), parts along dimension 0, may hold values from -6 to 6
- new_keys: bfloat16 [256, 1024], P(('rep', 'node'), 'tp'), parts along dimension 0, may hold values from -6 to 6
- new_values: bfloat16 [256, 1024], P(('rep', 'node'), 'tp'), parts along dimension 0, may hold values from -6 to 6
- lengths: int32 [256], P(('rep', 'node')), parts along dimension 0, may hold values from 2 to 384, as said below
- resid: bfloat16 [256, 6144], P(('rep', 'tp'), 'node'), parts along dimension 0, may hold values from -80 to 80
- wo: bfloat16 [6144, 6144], P('tp', 'node'), may hold values from -0.078125 to 0.078125
- norm_gain: float32 [6144], P('node'), may hold values from 0.1 to 1.9
- routes: int32 [256, 2], P('rep'), parts along dimension 0, may hold values from 0 to 3, all different within a row; in each aligned block of 128 rows (0 to 127, 128 to 255, ...) at most 80 rows name the same one
- route_weights: float32 [256, 2], P('rep'), parts along dimension 0, may hold values from 0.2 to 1
- w_gate: bfloat16 [6144, 32768], P(None, ('node', 'tp')), may hold values from -0.078125 to 0.078125
- w_up: bfloat16 [6144, 32768], P(None, ('node', 'tp')), may hold values from -0.078125 to 0.078125
- w_down: bfloat16 [32768, 6144], P(('node', 'tp')), may hold values from -0.09375 to 0.09375
Outputs:
- mixed: bfloat16 [256, 6144], P(('rep', 'tp'), 'node'), parts along dimension 0
There are 2 independent parts, one for each index of `rep`. A program takes and returns all parts, laid end to end along the dimension named above; an argument that names none is the same for every part. Nothing has to cross between parts.
Inputs may be any that keep to these rules, and one draw needn't show every extreme that they name: `routes`: each row names two different experts; over all 128 rows no expert is named by more than 80 rows, a bound that some block reaches. `lengths`: row 0 has exactly 384.
All inputs are finite; a program needn't handle non-finite values.
Results may differ from a plain program's by a relative error of at most 0.005.
Values may be sent and summed in bfloat16 or wider, within the bound.
A program may use at most 192 MiB of HBM per device.

v0:
```python
import jax
import jax.numpy as jnp
from jax import lax
from jax.sharding import PartitionSpec as P

D = 6144
HQ = 48
KVH = 8
HD = 128
FF = 8192
CTX = 384


EPSILON = 1e-05


def attend_block(queries, cache_keys, cache_values, new_keys, new_values, lengths):
    rows, kv_local = (cache_keys.shape[0], cache_keys.shape[1])
    groups = HQ // KVH
    factor = HD ** (-0.5)
    query_heads = queries.reshape(rows, kv_local, groups, HD)
    scores = (
        jnp.einsum("rkgd,rkpd->rkgp", query_heads, cache_keys, preferred_element_type=jnp.float32)
        * factor
    )
    valid = jnp.arange(CTX, dtype=jnp.int32)[None, :] < lengths[:, None]
    scores = jnp.where(valid[:, None, None, :], scores, -jnp.inf)
    key_heads = new_keys.reshape(rows, kv_local, HD)
    score_new = (
        jnp.einsum("rkgd,rkd->rkg", query_heads, key_heads, preferred_element_type=jnp.float32)
        * factor
    )
    highest = jnp.maximum(jnp.max(scores, axis=-1), score_new)
    exp_cache = jnp.exp(scores - highest[..., None])
    exp_new = jnp.exp(score_new - highest)
    totals = jnp.sum(exp_cache, axis=-1) + exp_new
    probs_cache = (exp_cache / totals[..., None]).astype(jnp.bfloat16)
    probs_new = (exp_new / totals).astype(jnp.bfloat16)
    attended = jnp.einsum(
        "rkgp,rkpd->rkgd", probs_cache, cache_values, preferred_element_type=jnp.float32
    )
    attended = attended + probs_new.astype(jnp.float32)[..., None] * new_values.reshape(
        rows, kv_local, 1, HD
    ).astype(jnp.float32)
    return attended.reshape(rows, kv_local * groups * HD).astype(jnp.bfloat16)


def local(
    queries,
    cache_keys,
    cache_values,
    new_keys,
    new_values,
    lengths,
    resid,
    wo,
    norm_gain,
    routes,
    route_weights,
    w_gate,
    w_up,
    w_down,
):
    attended = attend_block(queries, cache_keys, cache_values, new_keys, new_values, lengths)
    gathered = lax.all_gather(attended, "node", axis=0, tiled=True)
    projected = lax.psum_scatter(
        jnp.dot(gathered, wo, preferred_element_type=jnp.float32),
        "tp",
        scatter_dimension=0,
        tiled=True,
    )
    hidden = resid.astype(jnp.float32) + projected
    squares = lax.psum(jnp.sum(hidden * hidden, axis=1), "node")
    normed = (hidden * lax.rsqrt(squares / D + EPSILON)[:, None] * norm_gain[None, :]).astype(
        jnp.bfloat16
    )
    all_rows = lax.all_gather(normed, "tp", axis=0, tiled=True)
    device = lax.axis_index("node") * lax.axis_size("tp") + lax.axis_index("tp")
    hidden_local = w_gate.shape[1]
    expert = device * hidden_local // FF
    expert_weight = jnp.sum(jnp.where(routes == expert, route_weights, 0.0), axis=1)
    full_rows = lax.all_gather(all_rows, "node", axis=1, tiled=True)
    gate = jnp.dot(full_rows, w_gate, preferred_element_type=jnp.float32)
    upward = jnp.dot(full_rows, w_up, preferred_element_type=jnp.float32)
    activ = (jax.nn.silu(gate) * upward).astype(jnp.bfloat16)
    weighted = jnp.dot(activ, w_down, preferred_element_type=jnp.float32) * expert_weight[:, None]
    slices = lax.psum_scatter(
        weighted.astype(jnp.bfloat16), "node", scatter_dimension=1, tiled=True
    ).astype(jnp.float32)
    moe_part = lax.psum_scatter(slices, "tp", scatter_dimension=0, tiled=True)
    return (hidden + moe_part).astype(jnp.bfloat16)


def solution(mesh):
    return jax.shard_map(
        local,
        mesh=mesh,
        in_specs=(
            P(("rep", "node"), "tp"),
            P(("rep", "node"), "tp", None, None),
            P(("rep", "node"), "tp", None, None),
            P(("rep", "node"), "tp"),
            P(("rep", "node"), "tp"),
            P(("rep", "node")),
            P(("rep", "tp"), "node"),
            P("tp", "node"),
            P("node"),
            P("rep", None),
            P("rep", None),
            P(None, ("node", "tp")),
            P(None, ("node", "tp")),
            P(("node", "tp"), None),
        ),
        out_specs=P(("rep", "tp"), "node"),
        check_vma=False,
    )
```

profile of v0, /device:TPU:0, one launch (start us, length us, event | category | flops | bytes accessed | tf_op | source)
XLA Modules:
  0.0 190.2 jit_solution(18154991271827679628)
XLA Ops:
  6.5 0.0 reduce-scatter.4.cloned.1.call-start
  6.5 0.7 iota_compare_fusion
  7.3 0.7 reshape.47
  8.0 0.7 reshape.43
  8.7 1.0 reshape.41
  9.8 0.0 copy-start.6
  9.8 0.2 fusion.18
  10.0 5.3 %fusion.17 = (f32[32,2,6]{2,1,0:T(2,128)S(1)}, f32[32,2,6,384]{3,2,1,0:T(8,128)S(1)}) fusion(bf16[32,2,6,128]{3,2,1,0:T(8,128)(2,1)S(1)} %reshape.41, bf16[32,2,384,128]{3,2,1,0:T(8,128)(2,1)} %param.15, pred[32,384]{1,0:T(8,128)(4,1)S(1)} %iota_compare_fusion), kind=kOutput, calls=%fused_computation.33 | convolution fusion | flops 38190720 | bytes 6993408 | tf_op jit(solution)/shard_map/rkgd,rkpd->rkgp/dot_general | solution.py:23
  15.3 0.3 fusion.9
  15.6 0.1 fusion.13
  15.7 0.0 copy-done.6
  15.7 0.0 copy-start.2
  15.7 0.0 copy-start.3
  15.7 1.3 fusion.3
  17.0 0.0 copy-start.4
  17.0 0.0 copy-start.5
  17.0 0.1 convert_element_type.51
  17.2 7.9 %all_gather.9 = bf16[128,1536]{1,0:T(8,128)(2,1)S(1)} all-gather(bf16[32,1536]{1,0:T(8,128)(2,1)S(1)} %convert_element_type.51), channel_id=1, replica_groups=mesh['rep'=2,'node'=4,'tp'=4] {'node'}, dimensions={0}, use_global_device_ids=true | all-gather | bytes 491520 | tf_op jit(solution)/shard_map/all_gather | solution.py:65
  25.1 4.0 %fusion.19 = f32[128,1536]{1,0:T(8,128)} fusion(bf16[128,1536]{1,0:T(8,128)(2,1)S(1)} %all_gather.9, bf16[1536,1536]{1,0:T(8,128)(2,1)} %param.21), kind=kOutput, calls=%fused_computation.35 | convolution fusion | flops 603979776 | bytes 5898240 | tf_op jit(solution)/shard_map/dot_general | solution.py:67
  29.1 0.0 reduce-scatter.4.cloned.1.call-update
  29.1 0.0 all-gather.2.cloned.1.call-start
  29.2 24.4 %reduce-scatter.4.cloned.1.call-done = f32[32,1536]{1,0:T(8,128)} async-done(((f32[128,1536]{1,0:T(8,128)}), f32[32,1536]{1,0:T(8,128)}) %reduce-scatter.4.cloned.1.call-update) | async-done | bytes 196624 | tf_op jit(solution)/shard_map/reduce_scatter | solution.py:66
  53.5 0.0 copy-done.2
  53.5 1.1 multiply_reduce_fusion
  54.6 5.7 %psum.7 = f32[32]{0:T(128)S(1)} all-reduce(f32[32]{0:T(128)S(1)} %multiply_reduce_fusion), channel_id=1, replica_groups=mesh['rep'=2,'node'=4,'tp'=4] {'node'}, use_global_device_ids=true, to_apply=%region_4.5 | all-reduce | flops 32 | bytes 256 | tf_op jit(solution)/shard_map/psum | solution.py:73
  60.3 0.0 copy-done.3
  60.3 1.0 multiply_convert_fusion
  61.3 15.0 %all_gather.10 = bf16[128,1536]{1,0:T(8,128)(2,1)} all-gather(bf16[32,1536]{1,0:T(8,128)(2,1)S(1)} %multiply_convert_fusion), channel_id=1, replica_groups=mesh['rep'=2,'node'=4,'tp'=4] {'tp'}, dimensions={0}, use_global_device_ids=true | all-gather | bytes 491520 | tf_op jit(solution)/shard_map/all_gather | solution.py:77
  76.3 0.0 all-gather.2.cloned.1.call-update
  76.3 0.0 reduce-scatter.6.cloned.1.call-start
  76.4 0.0 copy-done.4
  76.4 0.0 copy-done.5
  76.4 19.4 %all-gather.2.cloned.1.call-done = bf16[128,6144]{1,0:T(8,128)(2,1)} async-done(((bf16[128,1536]{1,0:T(8,128)(2,1)}), bf16[128,6144]{1,0:T(8,128)(2,1)}) %all-gather.2.cloned.1.call-update) | async-done | bytes 1572880 | tf_op jit(solution)/shard_map/all_gather | solution.py:82
  95.8 0.0 copy-start
  95.8 12.0 %fusion.20 = f32[128,2048]{1,0:T(8,128)S(1)} fusion(bf16[128,6144]{1,0:T(8,128)(2,1)} %all-gather.2.cloned.1.call-done, bf16[6144,2048]{1,0:T(8,128)(2,1)} %param.25), kind=kOutput, calls=%fused_computation.36 | convolution fusion | flops 3221225472 | bytes 27787264 | tf_op jit(solution)/shard_map/dot_general | solution.py:83
  107.8 0.0 copy-done
  107.9 0.0 copy-start.1
  107.9 20.3 %fusion = bf16[128,6144]{1,0:T(8,128)(2,1)} fusion(bf16[2048,6144]{1,0:T(8,128)(2,1)} %param.27, bf16[128,6144]{1,0:T(8,128)(2,1)S(1)} %copy-done, bf16[6144,2048]{1,0:T(8,128)(2,1)} %param.26, f32[128]{0:T(128)S(1)} %fusion.14, f32[128,2048]{1,0:T(8,128)S(1)} %fusion.20), kind=kOutput, calls=%fused_computation.1 | convolution fusion | flops 6445596672 | bytes 54526464 | tf_op jit(solution)/shard_map/dot_general | solution.py:86
  128.2 0.0 reduce-scatter.6.cloned.1.call-update
  128.2 0.0 reduce-scatter.8.cloned.1.call-start
  128.3 28.3 %reduce-scatter.6.cloned.1.call-done = bf16[128,1536]{1,0:T(8,128)(2,1)} async-done(((bf16[128,6144]{1,0:T(8,128)(2,1)}), bf16[128,1536]{1,0:T(8,128)(2,1)}) %reduce-scatter.6.cloned.1.call-update) | async-done | bytes 393232 | tf_op jit(solution)/shard_map/reduce_scatter | solution.py:87
  156.5 1.9 %convert_element_type.55 = f32[128,1536]{1,0:T(8,128)} convert(bf16[128,1536]{1,0:T(8,128)(2,1)} %reduce-scatter.6.cloned.1.call-done) | non-fusion elementwise | flops 196608 | bytes 1179648 | tf_op jit(solution)/shard_map/convert_element_type | solution.py:89
  158.5 0.0 reduce-scatter.8.cloned.1.call-update
  158.5 23.6 %reduce-scatter.8.cloned.1.call-done = f32[32,1536]{1,0:T(8,128)} async-done(((f32[128,1536]{1,0:T(8,128)}), f32[32,1536]{1,0:T(8,128)}) %reduce-scatter.8.cloned.1.call-update) | async-done | bytes 196624 | tf_op jit(solution)/shard_map/reduce_scatter | solution.py:90
  182.1 0.0 copy-done.1
  182.1 1.6 add_convert_fusion
  (3 shorter events, 0.1 us)
Async XLA Ops:
  6.5 47.0 %reduce-scatter.4.cloned.1.call-start = ((), (), s32[]{:S(2)}) async-start(), calls=%async_computation.3 | async-start | bytes 983040 | tf_op jit(solution)/shard_map/reduce_scatter | solution.py:66
  9.8 5.9 %copy-start.6 = (bf16[32,2,384,128]{3,2,1,0:T(8,128)(2,1)S(1)}, bf16[32,2,384,128]{3,2,1,0:T(8,128)(2,1)}, u32[]{:S(2)}) copy-start(bf16[32,2,384,128]{3,2,1,0:T(8,128)(2,1)} %param.16) | copy-start | bytes 18874372
  15.7 37.8 %copy-start.2 = (bf16[32,1536]{1,0:T(8,128)(2,1)S(1)}, bf16[32,1536]{1,0:T(8,128)(2,1)}, u32[]{:S(2)}) copy-start(bf16[32,1536]{1,0:T(8,128)(2,1)} %param.20) | copy-start | bytes 294916
  15.7 44.5 %copy-start.3 = (f32[1536]{0:T(1024)S(1)}, f32[1536]{0:T(1024)}, u32[]{:S(2)}) copy-start(f32[1536]{0:T(1024)} %param.22) | copy-start | bytes 18436
  17.0 59.4 %copy-start.4 = (f32[128,2]{0,1:T(2,128)S(1)}, f32[128,2]{0,1:T(2,128)}, u32[]{:S(2)}) copy-start(f32[128,2]{0,1:T(2,128)} %param.24) | copy-start | bytes 3076
  17.0 59.4 %copy-start.5 = (s32[128,2]{0,1:T(2,128)S(1)}, s32[128,2]{0,1:T(2,128)}, u32[]{:S(2)}) copy-start(s32[128,2]{0,1:T(2,128)} %param.23) | copy-start | bytes 3076
  29.1 66.7 %all-gather.2.cloned.1.call-start = ((), (), s32[]{:S(2)}) async-start(), calls=%async_computation.4 | async-start | bytes 1966080 | tf_op jit(solution)/shard_map/all_gather | solution.py:82
  76.3 80.2 %reduce-scatter.6.cloned.1.call-start = ((), (), s32[]{:S(2)}) async-start(), calls=%async_computation.5 | async-start | bytes 1966080 | tf_op jit(solution)/shard_map/reduce_scatter | solution.py:87
  95.8 12.0 %copy-start = (bf16[128,6144]{1,0:T(8,128)(2,1)S(1)}, bf16[128,6144]{1,0:T(8,128)(2,1)}, u32[]{:S(2)}) copy-start(bf16[128,6144]{1,0:T(8,128)(2,1)} %all-gather.2.cloned.1.call-done) | copy-start | bytes 4718596
  107.9 74.3 %copy-start.1 = (f32[32,1536]{1,0:T(8,128)S(1)}, f32[32,1536]{1,0:T(8,128)}, u32[]{:S(2)}) copy-start(f32[32,1536]{1,0:T(8,128)} %reduce-scatter.4.cloned.1.call-done) | copy-start | bytes 589828
  128.2 53.9 %reduce-scatter.8.cloned.1.call-start = ((), (), s32[]{:S(2)}) async-start(), calls=%async_computation.6 | async-start | bytes 983040 | tf_op jit(solution)/shard_map/reduce_scatter | solution.py:90
Sparse Core Ops, SparseCore 0:
  29.2 24.2 reduce-scatter.3
  76.4 19.3 all-gather.1
  128.3 28.1 reduce-scatter.5
  158.8 23.2 reduce-scatter.7
where the time goes:
time: 191 us; the launch traced here: 190 us
  waiting for transfers between devices  95.7 us (50%)
  matrix products  43.1 us (23%)
  blocking collectives  28.6 us (15%)
  between operations  13.3 us (7%)
  other arithmetic  6.77 us (4%)
  local copies, waits for them, and re-layouts  2.66 us (1%)
    reduce_scatter x1, waiting for transfers between devices, local(): lax.psum_scatter(weighted.astype(jnp.bfloat16), 'node', scatter_dimension...  28.3 us
    reduce_scatter x1, waiting for transfers between devices, local(): lax.psum_scatter(jnp.dot(gathered, wo, preferred_element_type=jnp.float32...  24.4 us
    reduce_scatter x1, waiting for transfers between devices, local(): moe_part = lax.psum_scatter(slices, 'tp', scatter_dimension=0, tiled=True)  23.6 us
    dot_general x1, matrix products, local(): jnp.dot(activ, w_down, preferred_element_type=jnp.float32)  20.3 us
    all_gather x1, waiting for transfers between devices, local(): full_rows = lax.all_gather(all_rows, 'node', axis=1, tiled=True)  19.4 us
    all_gather x1, blocking collectives, local(): all_rows = lax.all_gather(normed, 'tp', axis=0, tiled=True)  15 us
    dot_general x1, matrix products, local(): gate = jnp.dot(full_rows, w_gate, preferred_element_type=jnp.float32)  12 us
    all_gather x1, blocking collectives, local(): gathered = lax.all_gather(attended, 'node', axis=0, tiled=True)  7.94 us
  transfers between devices with their start and end apart: 4, of which 4 were waited for; matrix products, arithmetic and copies ran while one was open for 0% of the time, Pallas kernels for 0%

commit v1 on v0

--- a/solution.py
+++ b/solution.py
@@ -1,6 +1,10 @@
+import functools
+
 import jax
 import jax.numpy as jnp
 from jax import lax
+from jax.experimental import pallas as pl
+from jax.experimental.pallas import tpu as pltpu
 from jax.sharding import PartitionSpec as P
 
 D = 6144
@@ -43,6 +47,385 @@
         rows, kv_local, 1, HD
     ).astype(jnp.float32)
     return attended.reshape(rows, kv_local * groups * HD).astype(jnp.bfloat16)
+
+
+DEPTH = 2048
+CHUNK = 512
+MESH = pl.DeviceIdType.MESH
+
+
+def layer_kernel(
+    T,
+    att_ref,
+    resid_ref,
+    gain_ref,
+    routes_ref,
+    rw_ref,
+    wo_hbm,
+    wg_hbm,
+    wu_hbm,
+    wd_hbm,
+    out_ref,
+    w_buf,
+    att_all,
+    full,
+    hidden,
+    act,
+    acc,
+    proj_send,
+    proj_recv,
+    sq_node,
+    sq_all,
+    sib_send,
+    sib_recv,
+    y_send,
+    y_recv,
+    z_recv,
+    w_sem,
+    att_s,
+    att_r,
+    pr_s,
+    pr_r,
+    sqn_s,
+    sqn_r,
+    sqt_s,
+    sqt_r,
+    ag_z_s,
+    ag_y_s,
+    ag_c_s,
+    ag_r,
+    sib_s,
+    sib_r,
+    y_s,
+    y_r,
+    z_s,
+    z_r,
+):
+    N = 4
+    R, F = resid_ref.shape
+    r = lax.axis_index("rep")
+    n = lax.axis_index("node")
+    t = lax.axis_index("tp")
+    y = n // 2
+    core = n % 2
+    ny = (n + 2) % N
+    ns = y * 2 + (core + 1) % 2
+    nd = (ns + 2) % N
+    SLOTS = w_buf.shape[0]
+    KB = D // DEPTH
+    per_c = 2 * KB
+    chunks = wg_hbm.shape[1] // CHUNK
+    wo_first = SLOTS - F // CHUNK
+
+    def tpeer(d):
+        return (t + d) % T
+
+    def npeer(d):
+        return (n + d) % N
+
+    def rows(i):
+        return pl.ds(pl.multiple_of(i * R, R), R)
+
+    def feats(i):
+        return pl.ds(pl.multiple_of(i * F, F), F)
+
+    def gu_copy(slot):
+        c, k = slot // per_c, slot % per_c
+        hbm = wg_hbm if k < KB else wu_hbm
+        return pltpu.make_async_copy(
+            hbm.at[pl.ds((k % KB) * DEPTH, DEPTH), pl.ds(c * CHUNK, CHUNK)],
+            w_buf.at[slot],
+            w_sem.at[slot],
+        )
+
+    def dest(q):
+        return ((y + 1 - q // 2) % 2) * 2 + (core + 1 - q % 2) % 2
+
+    def down_copy(i):
+        col = dest(i // (F // CHUNK)) * F + (i % (F // CHUNK)) * CHUNK
+        return pltpu.make_async_copy(
+            wd_hbm.at[:, pl.ds(pl.multiple_of(col, CHUNK), CHUNK)], w_buf.at[i], w_sem.at[i]
+        )
+
+    def wo_copy(j):
+        return pltpu.make_async_copy(
+            wo_hbm.at[:, pl.ds(j * CHUNK, CHUNK)],
+            w_buf.at[wo_first + j, pl.ds(0, F)],
+            w_sem.at[wo_first + j],
+        )
+
+    def remote(src, dst, ss, rs, node, tp):
+        return pltpu.make_async_remote_copy(
+            src_ref=src,
+            dst_ref=dst,
+            send_sem=ss,
+            recv_sem=rs,
+            device_id=(r, node, tp),
+            device_id_type=MESH,
+        )
+
+    for j in range(F // CHUNK):
+        wo_copy(j).start()
+    for slot in range(wo_first):
+        gu_copy(slot).start()
+
+    barrier = pltpu.get_barrier_semaphore()
+    for d in range(1, N):
+        pl.semaphore_signal(barrier, inc=1, device_id=(r, npeer(d), t), device_id_type=MESH)
+    for d in range(1, T):
+        pl.semaphore_signal(barrier, inc=1, device_id=(r, n, tpeer(d)), device_id_type=MESH)
+    pl.semaphore_wait(barrier, N + T - 2)
+
+    sends = []
+
+    def send(*args):
+        copy = remote(*args)
+        copy.start()
+        sends.append(copy)
+
+    for d in (2, 1, 3):
+        send(att_ref, att_all.at[rows(n)], att_s.at[d], att_r.at[n], npeer(d), t)
+    att_all[rows(n), :] = att_ref[...]
+    for d in range(1, N):
+        p = npeer(d)
+        remote(att_ref, att_all.at[rows(p)], att_s.at[d], att_r.at[p], p, t).wait_recv()
+
+    for j in range(F // CHUNK):
+        wo_copy(j).wait()
+        part = jnp.dot(
+            att_all[...], w_buf[wo_first + j, :F, :], preferred_element_type=jnp.float32
+        )
+        acc[:, j * CHUNK : (j + 1) * CHUNK] = part
+        proj_send[:, j * CHUNK : (j + 1) * CHUNK] = part.astype(jnp.bfloat16)
+    for d in (2, 1, 3):
+        p = tpeer(d)
+        send(proj_send.at[rows(p)], proj_recv.at[t], pr_s.at[d], pr_r.at[t], n, p)
+    for slot in range(wo_first, SLOTS):
+        gu_copy(slot).start()
+    total = resid_ref[...].astype(jnp.float32) + acc[rows(t), :]
+    for d in range(1, T):
+        p = tpeer(d)
+        remote(
+            proj_send.at[rows(p)], proj_recv.at[p], pr_s.at[d], pr_r.at[p], n, p
+        ).wait_recv()
+        total = total + proj_recv[p].astype(jnp.float32)
+    hidden[...] = total
+
+    full[rows(t), feats(n)] = (total * gain_ref[...]).astype(jnp.bfloat16)
+    sq_node[n] = jnp.broadcast_to(jnp.sum(total * total, axis=1, keepdims=True), (R, 128))
+    for d in range(1, N):
+        send(sq_node.at[n], sq_node.at[n], sqn_s.at[d], sqn_r.at[n], npeer(d), t)
+
+    def block(nn, tt):
+        return full.at[rows(tt), feats(nn)]
+
+    own = block(n, t)
+    send(own, own, ag_y_s.at[0], ag_r.at[n, t], ny, t)
+    for d in (2, 1, 3):
+        send(own, own, ag_z_s.at[d], ag_r.at[n, t], n, tpeer(d))
+    send(own, own, ag_c_s.at[0, 0], ag_r.at[n, t], ns, t)
+
+    for d in range(1, N):
+        p = npeer(d)
+        remote(sq_node.at[n], sq_node.at[p], sqn_s.at[d], sqn_r.at[p], p, t).wait_recv()
+    sq_all[rows(t), :] = sq_node[0] + sq_node[1] + sq_node[2] + sq_node[3]
+    for d in range(1, T):
+        sq = sq_all.at[rows(t)]
+        send(sq, sq, sqt_s.at[d], sqt_r.at[t], n, tpeer(d))
+
+    def arrived(nn, tt):
+        remote(own, block(nn, tt), ag_y_s.at[0], ag_r.at[nn, tt], ny, t).wait_recv()
+
+    for d in (1, 3, 2):
+        p = tpeer(d)
+        b = block(n, p)
+        arrived(n, p)
+        send(b, b, ag_y_s.at[d], ag_r.at[n, p], ny, t)
+        send(b, b, ag_c_s.at[0, d], ag_r.at[n, p], ns, t)
+    for d in (0, 1, 3, 2):
+        p = tpeer(d)
+        b = block(ny, p)
+        arrived(ny, p)
+        send(b, b, ag_c_s.at[1, d], ag_r.at[ny, p], ns, t)
+    for d in range(T):
+        arrived(ns, tpeer(d))
+        arrived(nd, tpeer(d))
+    for d in range(1, T):
+        p = tpeer(d)
+        sq = sq_all.at[rows(p)]
+        remote(sq, sq, sqt_s.at[d], sqt_r.at[p], n, p).wait_recv()
+    inv = lax.rsqrt(sq_all[:, 0:1] / D + EPSILON)
+
+    def slot_wait(slot):
+        pltpu.make_async_copy(
+            wd_hbm.at[:, pl.ds(0, CHUNK)], w_buf.at[slot], w_sem.at[slot]
+        ).wait()
+
+    downs = D // CHUNK
+
+    def gate_up(c, carry):
+        base = c * per_c
+        both = []
+        for m in range(2):
+            s = None
+            for k in range(KB):
+                slot = base + m * KB + k
+                slot_wait(slot)
+                part = jnp.dot(
+                    full[:, k * DEPTH : (k + 1) * DEPTH],
+                    w_buf[slot],
+                    preferred_element_type=jnp.float32,
+                )
+                s = part if s is None else s + part
+            both.append(s * inv)
+        gate, up = both
+        act[:, pl.ds(pl.multiple_of(c * CHUNK, CHUNK), CHUNK)] = (
+            gate / (1.0 + jnp.exp(-gate)) * up
+        ).astype(jnp.bfloat16)
+
+        @pl.when(c < downs // per_c)
+        def _():
+            for k in range(per_c):
+                down_copy(base + k).start()
+
+        return carry
+
+    lax.fori_loop(0, chunks, gate_up, 0)
+
+    expert = (n * T + t) * wg_hbm.shape[1] // FF
+    weight = jnp.sum(jnp.where(routes_ref[...] == expert, rw_ref[...], 0.0), axis=1, keepdims=True)
+
+    def down(q, store):
+        def step(k, carry):
+            slot = q * (F // CHUNK) + k
+            slot_wait(slot)
+            part = jnp.dot(act[...], w_buf[slot], preferred_element_type=jnp.float32)
+            store(pl.ds(pl.multiple_of(k * CHUNK, CHUNK), CHUNK), part * weight)
+            return carry
+
+        lax.fori_loop(0, F // CHUNK, step, 0)
+
+    def to_sibling(h):
+        def store(cols, v):
+            sib_send[h, :, cols] = v.astype(jnp.bfloat16)
+
+        return store
+
+    def to_acc(cols, v):
+        acc[:, cols] = v
+
+    def sib_wait(h):
+        remote(
+            sib_send.at[h], sib_recv.at[h], sib_s.at[h], sib_r.at[h], ns, t
+        ).wait_recv()
+
+    down(0, to_sibling(0))
+    send(sib_send.at[0], sib_recv.at[0], sib_s.at[0], sib_r.at[0], ns, t)
+    down(1, to_acc)
+    sib_wait(0)
+    for d in (2, 1, 3, 0):
+        p = tpeer(d)
+        y_send[p] = (acc[rows(p), :] + sib_recv[0, rows(p), :].astype(jnp.float32)).astype(
+            jnp.bfloat16
+        )
+        send(y_send.at[p], y_recv.at[p], y_s.at[d], y_r.at[p], ny, t)
+    down(2, to_sibling(1))
+    send(sib_send.at[1], sib_recv.at[1], sib_s.at[1], sib_r.at[1], ns, t)
+    down(3, to_acc)
+    sib_wait(1)
+    mine = None
+    for d in (2, 1, 3, 0):
+        p = tpeer(d)
+        remote(y_send.at[p], y_recv.at[p], y_s.at[d], y_r.at[p], ny, t).wait_recv()
+        s = (
+            acc[rows(p), :]
+            + sib_recv[1, rows(p), :].astype(jnp.float32)
+            + y_recv[p].astype(jnp.float32)
+        )
+        if d == 0:
+            mine = s + hidden[...]
+        else:
+            y_recv[p] = s.astype(jnp.bfloat16)
+            send(y_recv.at[p], z_recv.at[t], z_s.at[d], z_r.at[t], n, p)
+    for d in (1, 3, 2):
+        p = tpeer(d)
+        remote(y_recv.at[p], z_recv.at[p], z_s.at[d], z_r.at[p], n, p).wait_recv()
+        mine = mine + z_recv[p].astype(jnp.float32)
+    out_ref[...] = mine.astype(jnp.bfloat16)
+    for copy in sends:
+        copy.wait_send()
+
+
+def fused_layer(
+    attended, resid, wo, norm_gain, routes, route_weights, w_gate, w_up, w_down, tp
+):
+    R, F = resid.shape
+    rows = routes.shape[0]
+    bf, f32 = jnp.bfloat16, jnp.float32
+    vm = pl.BlockSpec(memory_space=pltpu.VMEM)
+    hbm = pl.BlockSpec(memory_space=pl.ANY)
+    slots = 2 * (D // DEPTH) * (w_gate.shape[1] // CHUNK)
+    dma = pltpu.SemaphoreType.DMA
+    return pl.pallas_call(
+        functools.partial(layer_kernel, tp),
+        out_shape=jax.ShapeDtypeStruct((R, F), bf),
+        in_specs=[vm] * 5 + [hbm] * 4,
+        out_specs=vm,
+        scratch_shapes=[
+            pltpu.VMEM((slots, DEPTH, CHUNK), bf),
+            pltpu.VMEM((rows, F), bf),
+            pltpu.VMEM((rows, D), bf),
+            pltpu.VMEM((R, F), f32),
+            pltpu.VMEM((rows, w_gate.shape[1]), bf),
+            pltpu.VMEM((rows, F), f32),
+            pltpu.VMEM((rows, F), bf),
+            pltpu.VMEM((tp, R, F), bf),
+            pltpu.VMEM((4, R, 128), f32),
+            pltpu.VMEM((rows, 128), f32),
+            pltpu.VMEM((2, rows, F), bf),
+            pltpu.VMEM((2, rows, F), bf),
+            pltpu.VMEM((tp, R, F), bf),
+            pltpu.VMEM((tp, R, F), bf),
+            pltpu.VMEM((tp, R, F), bf),
+            dma((slots,)),
+            dma((4,)),
+            dma((4,)),
+            dma((tp,)),
+            dma((tp,)),
+            dma((4,)),
+            dma((4,)),
+            dma((tp,)),
+            dma((tp,)),
+            dma((tp,)),
+            dma((tp,)),
+            dma((2, tp)),
+            dma((4, tp)),
+            dma((2,)),
+            dma((2,)),
+            dma((tp,)),
+            dma((tp,)),
+            dma((tp,)),
+            dma((tp,)),
+        ],
+        compiler_params=pltpu.CompilerParams(
+            collective_id=0, has_side_effects=True, vmem_limit_bytes=60 * 1024 * 1024
+        ),
+        cost_estimate=pl.CostEstimate(
+            flops=2 * rows * D * w_gate.shape[1] * 3,
+            bytes_accessed=3 * D * w_gate.shape[1] * 2,
+            transcendentals=rows * w_gate.shape[1],
+        ),
+    )(
+        attended,
+        resid,
+        norm_gain.reshape(1, F),
+        routes,
+        route_weights,
+        wo,
+        w_gate,
+        w_up,
+        w_down,
+    )
 
 
 def local(
@@ -62,6 +445,19 @@
     w_down,
 ):
     attended = attend_block(queries, cache_keys, cache_values, new_keys, new_values, lengths)
+    if lax.axis_size("node") == 4 and lax.axis_size("tp") == 4:
+        return fused_layer(
+            attended,
+            resid,
+            wo,
+            norm_gain,
+            routes,
+            route_weights,
+            w_gate,
+            w_up,
+            w_down,
+            lax.axis_size("tp"),
+        )
     gathered = lax.all_gather(attended, "node", axis=0, tiled=True)
     projected = lax.psum_scatter(
         jnp.dot(gathered, wo, preferred_element_type=jnp.float32),

time: 191 us -> 86.6 us (0.45)
  waiting for transfers between devices: 95.7 us -> 0 us
  Pallas kernels: 0 us -> 70.2 us
  matrix products: 43.1 us -> 9.39 us
  blocking collectives: 28.6 us -> 0 us
  between operations: 13.3 us -> 0.1 us
  other arithmetic: 6.77 us -> 1.13 us
  local copies, waits for them, and re-layouts: 2.66 us -> 5.48 us
    reduce_scatter x3 -> x0, waiting for transfers between devices: 76.2 us -> none  [the longest x1 28.3 us: local(): lax.psum_scatter(weighted.astype(jnp.bfloat16), 'node', scatter_dimension...]
    pallas_call x0 -> x1, Pallas kernels: none -> 70.2 us  [fused_layer(): pl.pallas_call(functools.partial(layer_kernel, tp), out_shape=jax.ShapeDt...]
    dot_general x3 -> x0, matrix products: 36.3 us -> none  [the longest x1 20.3 us: local(): jnp.dot(activ, w_down, preferred_element_type=jnp.float32)]
    all_gather x2 -> x0, blocking collectives: 22.9 us -> none  [the longest x1 15 us: local(): all_rows = lax.all_gather(normed, 'tp', axis=0, tiled=True)]
    all_gather x1 -> x0, waiting for transfers between devices: 19.4 us -> none  [local(): full_rows = lax.all_gather(all_rows, 'node', axis=1, tiled=True)]
    psum x1 -> x0, blocking collectives: 5.66 us -> none  [local(): squares = lax.psum(jnp.sum(hidden * hidden, axis=1), 'node')]
    convert_element_type x3 -> x0, other arithmetic: 4.56 us -> none  [the longest x1 1.95 us: local(): slices = lax.psum_scatter(weighted.astype(jnp.bfloat16), 'node', scatter_...]
    unnamed x14 -> x13, local copies, waits for them, and re-layouts: 0.04 us -> 3.03 us
  transfers between devices with their start and end apart: 4 -> 0, of which waited for: 4 -> 0; matrix products, arithmetic and copies ran while one was open for 0% -> 0% of each run, Pallas kernels for 0% -> 0%
where the time goes in v1:
time: 86.6 us; the launch traced here: 86.3 us
  Pallas kernels  70.2 us (81%)
  matrix products  9.39 us (11%)
  local copies, waits for them, and re-layouts  5.48 us (6%)
  other arithmetic  1.13 us (1%)
    pallas_call x1, Pallas kernels, fused_layer(): pl.pallas_call(functools.partial(layer_kernel, tp), out_shape=jax.ShapeDt...  70.2 us
    dot_general x1, matrix products, attend_block(): jnp.einsum('rkgd,rkpd->rkgp', query_heads, cache_keys, preferred_element_...  5.16 us
    dot_general x1, matrix products, attend_block(): jnp.einsum('rkgp,rkpd->rkgd', probs_cache, cache_values, preferred_elemen...  4.03 us
    unnamed x13, local copies, waits for them, and re-layouts  3.03 us

profile of v1, /device:TPU:0, one launch (start us, length us, event | category | flops | bytes accessed | tf_op | source)
XLA Modules:
  0.0 86.3 jit_solution(11929104123741282032)
XLA Ops:
  0.0 0.0 copy-start
  0.0 0.0 copy-start.1
  0.0 1.0 %reshape.41 = bf16[32,2,6,128]{3,2,1,0:T(8,128)(2,1)S(1)} reshape(bf16[32,1536]{1,0:T(8,128)(2,1)} %param.14) | data formatting | bytes 196608 | tf_op jit(solution)/shard_map/reshape | solution.py:25
  1.0 0.7 iota_compare_fusion
  1.8 5.2 %fusion.7 = (f32[32,2,6]{2,1,0:T(2,128)S(1)}, f32[32,2,6,384]{3,2,1,0:T(8,128)S(1)}) fusion(bf16[32,2,6,128]{3,2,1,0:T(8,128)(2,1)S(1)} %reshape.41, bf16[32,2,384,128]{3,2,1,0:T(8,128)(2,1)} %param.15, pred[32,384]{1,0:T(8,128)(4,1)S(1)} %iota_compare_fusion), kind=kOutput, calls=%fused_computation.15 | convolution fusion | flops 38190720 | bytes 6993408 | tf_op jit(solution)/shard_map/rkgd,rkpd->rkgp/dot_general | solution.py:27
  6.9 0.0 copy-start.3
  7.0 0.0 copy-start.4
  7.0 0.0 copy-start.2
  7.0 0.0 copy-done
  7.0 0.2 fusion.8
  7.3 0.3 fusion.2
  7.6 0.1 fusion.5
  7.6 0.0 copy-done.1
  7.7 4.0 %fusion.1 = bf16[32,2,6,128]{3,2,1,0:T(8,128)(2,1)S(1)} fusion(bf16[32,2,384,128]{3,2,1,0:T(8,128)(2,1)} %param.16, f32[32,2,6,384]{3,2,1,0:T(8,128)S(1)} %get-tuple-element.8, f32[32,2,6]{2,1,0:T(2,128)S(1)} %get-tuple-element.6, f32[32,2,6]{2,1,0:T(2,128)S(1)} %multiply_maximum_fusion, f32[32,2,128]{2,1,0:T(2,128)S(1)} %reshape.44, ...), kind=kOutput, calls=%fused_computation.3 | convolution fusion | flops 38338560 | bytes 7016960 | tf_op jit(solution)/shard_map/rkgp,rkpd->rkgd/dot_general | solution.py:43
  11.7 0.8 convert_element_type.31.att_ref
  12.5 0.0 copy-done.3
  12.5 0.7 copy.17.routes_ref
  13.2 0.0 copy-done.4
  13.2 0.7 copy.18.rw_ref
  13.9 0.0 copy-done.2
  13.9 0.6 reshape.43.gain_ref
  14.5 70.2 %shard_map.136 = bf16[32,1536]{1,0:T(8,128)(2,1)} custom-call(bf16[32,1536]{1,0:T(8,128)(2,1)} %convert_element_type.31.att_ref, bf16[32,1536]{1,0:T(8,128)(2,1)} %resid_ref.1, f32[1,1536]{1,0:T(1,128)} %reshape.43.gain_ref, s32[128,2]{1,0:T(8,128)} %copy.17.routes_ref, f32[128,2]{1,0:T(8,128)} %copy.18.rw_ref, bf16[1536,1536]{1,0:T(8,128)(2,1)} %wo_hbm.1, ...), custom_call_target="tpu_custom_call" | custom-call | flops 9663676416 | bytes 75497472 | tf_op jit(solution)/shard_map/pallas_call | solution.py:369
  84.7 1.5 %copy.22 = bf16[32,1536]{1,0:T(8,128)(2,1)} copy(bf16[32,1536]{1,0:T(8,128)(2,1)} %shard_map.136) | data formatting | bytes 196608
  (3 shorter events, 0.1 us)
Async XLA Ops:
  0.0 7.0 %copy-start = (bf16[32,256]{1,0:T(8,128)(2,1)S(1)}, bf16[32,256]{1,0:T(8,128)(2,1)}, u32[]{:S(2)}) copy-start(bf16[32,256]{1,0:T(8,128)(2,1)} %param.17) | copy-start | bytes 49156
  0.0 7.6 %copy-start.1 = (bf16[32,256]{1,0:T(8,128)(2,1)S(1)}, bf16[32,256]{1,0:T(8,128)(2,1)}, u32[]{:S(2)}) copy-start(bf16[32,256]{1,0:T(8,128)(2,1)} %param.18) | copy-start | bytes 49156
  6.9 5.5 %copy-start.3 = (s32[128,2]{0,1:T(2,128)S(1)}, s32[128,2]{0,1:T(2,128)}, u32[]{:S(2)}) copy-start(s32[128,2]{0,1:T(2,128)} %param.23) | copy-start | bytes 3076
  7.0 6.3 %copy-start.4 = (f32[128,2]{0,1:T(2,128)S(1)}, f32[128,2]{0,1:T(2,128)}, u32[]{:S(2)}) copy-start(f32[128,2]{0,1:T(2,128)} %param.24) | copy-start | bytes 3076
  7.0 7.0 %copy-start.2 = (f32[1536]{0:T(1024)S(1)}, f32[1536]{0:T(1024)}, u32[]{:S(2)}) copy-start(f32[1536]{0:T(1024)} %param.22) | copy-start | bytes 18436

commit v2 on v1

--- a/solution.py
+++ b/solution.py
@@ -56,17 +56,27 @@
 
 def layer_kernel(
     T,
-    att_ref,
+    q_ref,
+    nk_ref,
+    nv_ref,
+    len_ref,
     resid_ref,
     gain_ref,
     routes_ref,
     rw_ref,
+    ck_hbm,
+    cv_hbm,
     wo_hbm,
     wg_hbm,
     wu_hbm,
     wd_hbm,
     out_ref,
     w_buf,
+    q_s,
+    o_s,
+    nk_s,
+    nv_s,
+    att_ref,
     att_all,
     full,
     hidden,
@@ -82,6 +92,7 @@
     y_recv,
     z_recv,
     w_sem,
+    kv_sem,
     att_s,
     att_r,
     pr_s,
@@ -164,9 +175,28 @@
             device_id_type=MESH,
         )
 
+    KV = nk_ref.shape[1] // HD
+    G = HQ // KVH
+    PAIR = KV * CTX
+    RB = DEPTH // PAIR
+    LB = CHUNK // HD
+    kv_slots = R // (RB * LB)
+    k_first = wo_first - 2 * kv_slots
+    v_first = wo_first - kv_slots
+
+    def kv_copy(hbm, first, i):
+        return pltpu.make_async_copy(
+            hbm.at[pl.ds(i * RB * PAIR, RB * PAIR)],
+            w_buf.at[first + i // LB, pl.ds(0, RB * PAIR), pl.ds((i % LB) * HD, HD)],
+            kv_sem.at[(first - k_first) * LB + i],
+        )
+
+    for i in range(R // RB):
+        kv_copy(ck_hbm, k_first, i).start()
+        kv_copy(cv_hbm, v_first, i).start()
     for j in range(F // CHUNK):
         wo_copy(j).start()
-    for slot in range(wo_first):
+    for slot in range(k_first):
         gu_copy(slot).start()
 
     barrier = pltpu.get_barrier_semaphore()
@@ -175,6 +205,80 @@
     for d in range(1, T):
         pl.semaphore_signal(barrier, inc=1, device_id=(r, n, tpeer(d)), device_id_type=MESH)
     pl.semaphore_wait(barrier, N + T - 2)
+
+    q_s[...] = jnp.zeros_like(q_s)
+    for k in range(KV):
+        lanes = slice(k * HD, (k + 1) * HD)
+        nk_s[:, k, :] = nk_ref[:, lanes].astype(jnp.float32)
+        nv_s[:, k, :] = nv_ref[:, lanes].astype(jnp.float32)
+        for g in range(G):
+            h = k * G + g
+            q_s[:, 8 * k + g, :] = q_ref[:, h * HD : (h + 1) * HD].astype(jnp.float32)
+    positions = lax.broadcasted_iota(jnp.int32, (8 * KV, CTX), 1)
+    nt = (((1,), (1,)), ((), ()))
+
+    def per_head(ref, row):
+        return jnp.concatenate(
+            [jnp.broadcast_to(ref[row, k : k + 1, :], (8, HD)) for k in range(KV)], axis=0
+        )
+
+    def diagonal(parts):
+        return jnp.concatenate([p[8 * k : 8 * k + 8] for k, p in enumerate(parts)], axis=0)
+
+    def attend(s, carry):
+        for b in range(LB):
+            for first in (k_first, v_first):
+                pltpu.make_async_copy(
+                    ck_hbm.at[pl.ds(0, RB * PAIR)],
+                    w_buf.at[first + s, pl.ds(0, RB * PAIR), pl.ds(b * HD, HD)],
+                    kv_sem.at[(first - k_first) * LB + s * LB + b],
+                ).wait()
+        for b in range(LB):
+            lanes = slice(b * HD, (b + 1) * HD)
+            for i in range(RB):
+                row = (s * LB + b) * RB + i
+                q = q_s[row]
+                qb = q.astype(jnp.bfloat16)
+                scores = diagonal(
+                    [
+                        lax.dot_general(
+                            qb,
+                            w_buf[k_first + s, i * PAIR + k * CTX : i * PAIR + (k + 1) * CTX, lanes],
+                            nt,
+                            preferred_element_type=jnp.float32,
+                        )
+                        for k in range(KV)
+                    ]
+                )
+                scores = scores * HD ** (-0.5)
+                scores = jnp.where(positions < len_ref[row], scores, -jnp.inf)
+                new = jnp.sum(q * per_head(nk_s, row), axis=1, keepdims=True) * HD ** (-0.5)
+                highest = jnp.maximum(jnp.max(scores, axis=1, keepdims=True), new)
+                e = jnp.exp(scores - highest)
+                e_new = jnp.exp(new - highest)
+                scale = 1.0 / (jnp.sum(e, axis=1, keepdims=True) + e_new)
+                probs = (e * scale).astype(jnp.bfloat16)
+                p_new = (e_new * scale).astype(jnp.bfloat16).astype(jnp.float32)
+                o = diagonal(
+                    [
+                        jnp.dot(
+                            probs,
+                            w_buf[v_first + s, i * PAIR + k * CTX : i * PAIR + (k + 1) * CTX, lanes],
+                            preferred_element_type=jnp.float32,
+                        )
+                        for k in range(KV)
+                    ]
+                )
+                o_s[row] = o + p_new * per_head(nv_s, row)
+        return carry
+
+    lax.fori_loop(0, kv_slots, attend, 0)
+    for k in range(KV):
+        for g in range(G):
+            h = k * G + g
+            att_ref[:, h * HD : (h + 1) * HD] = o_s[:, 8 * k + g, :].astype(jnp.bfloat16)
+    for slot in range(k_first, wo_first):
+        gu_copy(slot).start()
 
     sends = []
 
@@ -357,22 +461,42 @@
 
 
 def fused_layer(
-    attended, resid, wo, norm_gain, routes, route_weights, w_gate, w_up, w_down, tp
+    queries,
+    cache_keys,
+    cache_values,
+    new_keys,
+    new_values,
+    lengths,
+    resid,
+    wo,
+    norm_gain,
+    routes,
+    route_weights,
+    w_gate,
+    w_up,
+    w_down,
+    tp,
 ):
     R, F = resid.shape
     rows = routes.shape[0]
     bf, f32 = jnp.bfloat16, jnp.float32
     vm = pl.BlockSpec(memory_space=pltpu.VMEM)
     hbm = pl.BlockSpec(memory_space=pl.ANY)
+    kv = cache_keys.shape[1]
     slots = 2 * (D // DEPTH) * (w_gate.shape[1] // CHUNK)
     dma = pltpu.SemaphoreType.DMA
     return pl.pallas_call(
         functools.partial(layer_kernel, tp),
         out_shape=jax.ShapeDtypeStruct((R, F), bf),
-        in_specs=[vm] * 5 + [hbm] * 4,
+        in_specs=[vm] * 3 + [pl.BlockSpec(memory_space=pltpu.SMEM)] + [vm] * 4 + [hbm] * 6,
         out_specs=vm,
         scratch_shapes=[
             pltpu.VMEM((slots, DEPTH, CHUNK), bf),
+            pltpu.VMEM((R, 8 * kv, HD), f32),
+            pltpu.VMEM((R, 8 * kv, HD), f32),
+            pltpu.VMEM((R, kv, HD), f32),
+            pltpu.VMEM((R, kv, HD), f32),
+            pltpu.VMEM(queries.shape, bf),
             pltpu.VMEM((rows, F), bf),
             pltpu.VMEM((rows, D), bf),
             pltpu.VMEM((R, F), f32),
@@ -388,6 +512,7 @@
             pltpu.VMEM((tp, R, F), bf),
             pltpu.VMEM((tp, R, F), bf),
             dma((slots,)),
+            dma((2 * (R // (DEPTH // (kv * CTX))),)),
             dma((4,)),
             dma((4,)),
             dma((tp,)),
@@ -416,11 +541,16 @@
             transcendentals=rows * w_gate.shape[1],
         ),
     )(
-        attended,
+        queries,
+        new_keys,
+        new_values,
+        lengths,
         resid,
         norm_gain.reshape(1, F),
         routes,
         route_weights,
+        cache_keys.reshape(-1, HD),
+        cache_values.reshape(-1, HD),
         wo,
         w_gate,
         w_up,
@@ -444,10 +574,14 @@
     w_up,
     w_down,
 ):
-    attended = attend_block(queries, cache_keys, cache_values, new_keys, new_values, lengths)
     if lax.axis_size("node") == 4 and lax.axis_size("tp") == 4:
         return fused_layer(
-            attended,
+            queries,
+            cache_keys,
+            cache_values,
+            new_keys,
+            new_values,
+            lengths,
             resid,
             wo,
             norm_gain,
@@ -458,6 +592,7 @@
             w_down,
             lax.axis_size("tp"),
         )
+    attended = attend_block(queries, cache_keys, cache_values, new_keys, new_values, lengths)
     gathered = lax.all_gather(attended, "node", axis=0, tiled=True)
     projected = lax.psum_scatter(
         jnp.dot(gathered, wo, preferred_element_type=jnp.float32),

time: 86.6 us -> 89.4 us (1.032)
  Pallas kernels: 70.2 us -> 83.5 us
  matrix products: 9.39 us -> 0 us
  other arithmetic: 1.13 us -> 0 us
    pallas_call x1, Pallas kernels: 70.2 us -> 83.5 us  [fused_layer(): pl.pallas_call(functools.partial(layer_kernel, tp), out_shape=jax.ShapeDt...]
    dot_general x3 -> x0, matrix products: 9.39 us -> none  [the longest x1 5.16 us: attend_block(): jnp.einsum('rkgd,rkpd->rkgp', query_heads, cache_keys, preferred_element_...]
    unnamed x13 -> x3, local copies, waits for them, and re-layouts: 3.03 us -> 4.35 us
    reshape x2 -> x0, local copies, waits for them, and re-layouts: 1.05 us -> none  [the longest x1 1.04 us: attend_block(): query_heads = queries.reshape(rows, kv_local, groups, HD)]
where the time goes in v2:
time: 89.4 us; the launch traced here: 89.1 us
  Pallas kernels  83.5 us (93%)
  local copies, waits for them, and re-layouts  5.64 us (6%)
    pallas_call x1, Pallas kernels, fused_layer(): pl.pallas_call(functools.partial(layer_kernel, tp), out_shape=jax.ShapeDt...  83.5 us
    unnamed x3, local copies, waits for them, and re-layouts  4.35 us

profile of v2, /device:TPU:0, one launch (start us, length us, event | category | flops | bytes accessed | tf_op | source)
XLA Modules:
  0.0 89.1 jit_solution(6069850476947456820)
XLA Ops:
  0.0 1.3 %reshape.9.gain_ref = f32[1,1536]{1,0:T(1,128)} reshape(f32[1536]{0:T(1024)} %param.22) | data formatting | bytes 12288 | tf_op jit(solution)/shard_map/reshape | solution.py:549
  1.3 1.4 %copy.15.routes_ref = s32[128,2]{1,0:T(8,128)} copy(s32[128,2]{0,1:T(2,128)} %param.23) | data formatting | bytes 2048 | tf_op args[9]
  2.7 1.4 %copy.16.rw_ref = f32[128,2]{1,0:T(8,128)} copy(f32[128,2]{0,1:T(2,128)} %param.24) | data formatting | bytes 2048 | tf_op args[10]
  4.1 83.5 %shard_map.136 = bf16[32,1536]{1,0:T(8,128)(2,1)} custom-call(bf16[32,1536]{1,0:T(8,128)(2,1)} %q_ref.1, bf16[32,256]{1,0:T(8,128)(2,1)} %nk_ref.1, bf16[32,256]{1,0:T(8,128)(2,1)} %nv_ref.1, s32[32]{0:T(128)} %len_ref.1, bf16[32,1536]{1,0:T(8,128)(2,1)} %resid_ref.1, f32[1,1536]{1,0:T(1,128)} %reshape.9.gain_ref, s32[128,2]{1,0:T(8,128)} %copy.15.routes_ref, ...), custom_call_target="tpu_custom_call" | custom-call | flops 9663676416 | bytes 75497472 | tf_op jit(solution)/shard_map/pallas_call | solution.py:488
  87.6 1.5 %copy.18 = bf16[32,1536]{1,0:T(8,128)(2,1)} copy(bf16[32,1536]{1,0:T(8,128)(2,1)} %shard_map.136) | data formatting | bytes 196608

commit v3 on v1

--- a/solution.py
+++ b/solution.py
@@ -49,7 +49,6 @@
     return attended.reshape(rows, kv_local * groups * HD).astype(jnp.bfloat16)
 
 
-DEPTH = 2048
 CHUNK = 512
 MESH = pl.DeviceIdType.MESH
 
@@ -67,6 +66,7 @@
     wd_hbm,
     out_ref,
     w_buf,
+    gu_acc,
     att_all,
     full,
     hidden,
@@ -112,9 +112,10 @@
     ns = y * 2 + (core + 1) % 2
     nd = (ns + 2) % N
     SLOTS = w_buf.shape[0]
-    KB = D // DEPTH
-    per_c = 2 * KB
     chunks = wg_hbm.shape[1] // CHUNK
+    per_k = 2 * chunks
+    order = (n, ns, ny, nd)
+    PARTS = F // CHUNK
     wo_first = SLOTS - F // CHUNK
 
     def tpeer(d):
@@ -130,10 +131,10 @@
         return pl.ds(pl.multiple_of(i * F, F), F)
 
     def gu_copy(slot):
-        c, k = slot // per_c, slot % per_c
-        hbm = wg_hbm if k < KB else wu_hbm
+        c = slot % per_k // 2
+        hbm = wu_hbm if slot % 2 else wg_hbm
         return pltpu.make_async_copy(
-            hbm.at[pl.ds((k % KB) * DEPTH, DEPTH), pl.ds(c * CHUNK, CHUNK)],
+            hbm.at[feats(order[slot // per_k]), pl.ds(c * CHUNK, CHUNK)],
             w_buf.at[slot],
             w_sem.at[slot],
         )
@@ -141,16 +142,20 @@
     def dest(q):
         return ((y + 1 - q // 2) % 2) * 2 + (core + 1 - q % 2) % 2
 
-    def down_copy(i):
-        col = dest(i // (F // CHUNK)) * F + (i % (F // CHUNK)) * CHUNK
-        return pltpu.make_async_copy(
-            wd_hbm.at[:, pl.ds(pl.multiple_of(col, CHUNK), CHUNK)], w_buf.at[i], w_sem.at[i]
-        )
+    def down_start(slot):
+        k = slot % chunks
+        for j in range(PARTS):
+            col = dest(slot // chunks) * F + j * CHUNK
+            pltpu.make_async_copy(
+                wd_hbm.at[pl.ds(k * CHUNK, CHUNK), pl.ds(pl.multiple_of(col, CHUNK), CHUNK)],
+                w_buf.at[slot, pl.ds(j * CHUNK, CHUNK)],
+                w_sem.at[slot],
+            ).start()
 
     def wo_copy(j):
         return pltpu.make_async_copy(
             wo_hbm.at[:, pl.ds(j * CHUNK, CHUNK)],
-            w_buf.at[wo_first + j, pl.ds(0, F)],
+            w_buf.at[wo_first + j],
             w_sem.at[wo_first + j],
         )
 
@@ -193,7 +198,7 @@
     for j in range(F // CHUNK):
         wo_copy(j).wait()
         part = jnp.dot(
-            att_all[...], w_buf[wo_first + j, :F, :], preferred_element_type=jnp.float32
+            att_all[...], w_buf[wo_first + j], preferred_element_type=jnp.float32
         )
         acc[:, j * CHUNK : (j + 1) * CHUNK] = part
         proj_send[:, j * CHUNK : (j + 1) * CHUNK] = part.astype(jnp.bfloat16)
@@ -211,7 +216,7 @@
         total = total + proj_recv[p].astype(jnp.float32)
     hidden[...] = total
 
-    full[rows(t), feats(n)] = (total * gain_ref[...]).astype(jnp.bfloat16)
+    full[rows(t), feats(n)] = (total * gain_ref[...][None, :]).astype(jnp.bfloat16)
     sq_node[n] = jnp.broadcast_to(jnp.sum(total * total, axis=1, keepdims=True), (R, 128))
     for d in range(1, N):
         send(sq_node.at[n], sq_node.at[n], sqn_s.at[d], sqn_r.at[n], npeer(d), t)
@@ -242,6 +247,39 @@
         arrived(n, p)
         send(b, b, ag_y_s.at[d], ag_r.at[n, p], ny, t)
         send(b, b, ag_c_s.at[0, d], ag_r.at[n, p], ns, t)
+
+    def slot_wait(slot):
+        pltpu.make_async_copy(
+            wo_hbm.at[:, pl.ds(0, CHUNK)], w_buf.at[slot], w_sem.at[slot]
+        ).wait()
+
+    def gate_up(k, finish=None):
+        def step(c, carry):
+            both = []
+            for m in range(2):
+                slot = k * per_k + c * 2 + m
+                slot_wait(slot)
+                part = jnp.dot(
+                    full[:, feats(order[k])], w_buf[slot], preferred_element_type=jnp.float32
+                )
+                if k > 0:
+                    part = gu_acc[c * 2 + m] + part
+                if finish is None:
+                    gu_acc[c * 2 + m] = part
+                both.append(part)
+            if finish is not None:
+                gate, up = both[0] * finish, both[1] * finish
+                act[:, pl.ds(pl.multiple_of(c * CHUNK, CHUNK), CHUNK)] = (
+                    gate / (1.0 + jnp.exp(-gate)) * up
+                ).astype(jnp.bfloat16)
+            return carry
+
+        lax.fori_loop(0, chunks, step, 0)
+        for slot in range(k * per_k, (k + 1) * per_k):
+            if slot < N * chunks:
+                down_start(slot)
+
+    gate_up(0)
     for d in (0, 1, 3, 2):
         p = tpeer(d)
         b = block(ny, p)
@@ -249,61 +287,42 @@
         send(b, b, ag_c_s.at[1, d], ag_r.at[ny, p], ns, t)
     for d in range(T):
         arrived(ns, tpeer(d))
+    gate_up(1)
+    gate_up(2)
+    for d in range(T):
         arrived(nd, tpeer(d))
     for d in range(1, T):
         p = tpeer(d)
         sq = sq_all.at[rows(p)]
         remote(sq, sq, sqt_s.at[d], sqt_r.at[p], n, p).wait_recv()
-    inv = lax.rsqrt(sq_all[:, 0:1] / D + EPSILON)
-
-    def slot_wait(slot):
-        pltpu.make_async_copy(
-            wd_hbm.at[:, pl.ds(0, CHUNK)], w_buf.at[slot], w_sem.at[slot]
-        ).wait()
-
-    downs = D // CHUNK
-
-    def gate_up(c, carry):
-        base = c * per_c
-        both = []
-        for m in range(2):
-            s = None
-            for k in range(KB):
-                slot = base + m * KB + k
-                slot_wait(slot)
+    gate_up(3, lax.rsqrt(sq_all[:, 0:1] / D + EPSILON))
+
+    expert = (n * T + t) * wg_hbm.shape[1] // FF
+    weight = jnp.sum(jnp.where(routes_ref[...] == expert, rw_ref[...], 0.0), axis=0, keepdims=True)
+    square = (weight.shape[1], weight.shape[1])
+    eye = lax.broadcasted_iota(jnp.int32, square, 0) == lax.broadcasted_iota(jnp.int32, square, 1)
+    weight = jnp.sum(
+        jnp.where(eye, jnp.broadcast_to(weight, square), 0.0), axis=1, keepdims=True
+    )
+
+    def down(q, store):
+        for k in range(chunks):
+            slot_wait(q * chunks + k)
+
+        def step(j, carry):
+            cols = pl.ds(pl.multiple_of(j * CHUNK, CHUNK), CHUNK)
+            total = None
+            for k in range(chunks):
                 part = jnp.dot(
-                    full[:, k * DEPTH : (k + 1) * DEPTH],
-                    w_buf[slot],
+                    act[:, k * CHUNK : (k + 1) * CHUNK],
+                    w_buf[q * chunks + k, cols, :],
                     preferred_element_type=jnp.float32,
                 )
-                s = part if s is None else s + part
-            both.append(s * inv)
-        gate, up = both
-        act[:, pl.ds(pl.multiple_of(c * CHUNK, CHUNK), CHUNK)] = (
-            gate / (1.0 + jnp.exp(-gate)) * up
-        ).astype(jnp.bfloat16)
-
-        @pl.when(c < downs // per_c)
-        def _():
-            for k in range(per_c):
-                down_copy(base + k).start()
-
-        return carry
-
-    lax.fori_loop(0, chunks, gate_up, 0)
-
-    expert = (n * T + t) * wg_hbm.shape[1] // FF
-    weight = jnp.sum(jnp.where(routes_ref[...] == expert, rw_ref[...], 0.0), axis=1, keepdims=True)
-
-    def down(q, store):
-        def step(k, carry):
-            slot = q * (F // CHUNK) + k
-            slot_wait(slot)
-            part = jnp.dot(act[...], w_buf[slot], preferred_element_type=jnp.float32)
-            store(pl.ds(pl.multiple_of(k * CHUNK, CHUNK), CHUNK), part * weight)
+                total = part if total is None else total + part
+            store(cols, total * weight)
             return carry
 
-        lax.fori_loop(0, F // CHUNK, step, 0)
+        lax.fori_loop(0, PARTS, step, 0)
 
     def to_sibling(h):
         def store(cols, v):
@@ -364,7 +383,8 @@
     bf, f32 = jnp.bfloat16, jnp.float32
     vm = pl.BlockSpec(memory_space=pltpu.VMEM)
     hbm = pl.BlockSpec(memory_space=pl.ANY)
-    slots = 2 * (D // DEPTH) * (w_gate.shape[1] // CHUNK)
+    chunks = w_gate.shape[1] // CHUNK
+    slots = 2 * (D // F) * chunks
     dma = pltpu.SemaphoreType.DMA
     return pl.pallas_call(
         functools.partial(layer_kernel, tp),
@@ -372,7 +392,8 @@
         in_specs=[vm] * 5 + [hbm] * 4,
         out_specs=vm,
         scratch_shapes=[
-            pltpu.VMEM((slots, DEPTH, CHUNK), bf),
+            pltpu.VMEM((slots, F, CHUNK), bf),
+            pltpu.VMEM((2 * chunks, rows, CHUNK), f32),
             pltpu.VMEM((rows, F), bf),
             pltpu.VMEM((rows, D), bf),
             pltpu.VMEM((R, F), f32),
@@ -418,9 +439,9 @@
     )(
         attended,
         resid,
-        norm_gain.reshape(1, F),
-        routes,
-        route_weights,
+        norm_gain,
+        routes.T,
+        route_weights.T,
         wo,
         w_gate,
         w_up,

time: 86.6 us -> 81.4 us (0.940)
  matrix products: 9.39 us -> 6.78 us
  Pallas kernels: 70.2 us -> 68.3 us
    dot_general x1, matrix products: 4.03 us -> 1.27 us  [attend_block(): jnp.einsum('rkgp,rkpd->rkgd', probs_cache, cache_values, preferred_elemen...]
    pallas_call x1, Pallas kernels: 70.2 us -> 68.3 us  [fused_layer(): pl.pallas_call(functools.partial(layer_kernel, tp), out_shape=jax.ShapeDt...]
    unnamed x13 -> x3, local copies, waits for them, and re-layouts: 3.03 us -> 1.55 us
where the time goes in v3:
time: 81.4 us; the launch traced here: 81.1 us
  Pallas kernels  68.3 us (84%)
  matrix products  6.78 us (8%)
  local copies, waits for them, and re-layouts  4.82 us (6%)
  other arithmetic  1.12 us (1%)
    pallas_call x1, Pallas kernels, fused_layer(): pl.pallas_call(functools.partial(layer_kernel, tp), out_shape=jax.ShapeDt...  68.3 us
    dot_general x1, matrix products, attend_block(): jnp.einsum('rkgd,rkpd->rkgp', query_heads, cache_keys, preferred_element_...  5.32 us

profile of v3, /device:TPU:0, one launch (start us, length us, event | category | flops | bytes accessed | tf_op | source)
XLA Modules:
  0.0 81.1 jit_solution(972866088086164702)
XLA Ops:
  0.0 0.7 iota_compare_fusion
  0.7 0.7 reshape.44
  1.5 0.7 reshape.40
  2.2 1.0 %reshape.38 = bf16[32,2,6,128]{3,2,1,0:T(8,128)(2,1)S(1)} reshape(bf16[32,1536]{1,0:T(8,128)(2,1)} %param.14) | data formatting | bytes 196608 | tf_op jit(solution)/shard_map/reshape | solution.py:25
  3.2 0.0 copy-start
  3.2 0.2 fusion.8
  3.4 5.3 %fusion.7 = (f32[32,2,6]{2,1,0:T(2,128)S(1)}, f32[32,2,6,384]{3,2,1,0:T(8,128)S(1)}) fusion(bf16[32,2,6,128]{3,2,1,0:T(8,128)(2,1)S(1)} %reshape.38, bf16[32,2,384,128]{3,2,1,0:T(8,128)(2,1)} %param.15, pred[32,384]{1,0:T(8,128)(4,1)S(1)} %iota_compare_fusion), kind=kOutput, calls=%fused_computation.15 | convolution fusion | flops 38190720 | bytes 6993408 | tf_op jit(solution)/shard_map/rkgd,rkpd->rkgp/dot_general | solution.py:27
  8.8 0.3 fusion.2
  9.1 0.1 fusion.5
  9.2 0.0 copy-done
  9.2 1.3 %fusion.1 = bf16[32,2,6,128]{3,2,1,0:T(8,128)(2,1)S(1)} fusion(bf16[32,2,384,128]{3,2,1,0:T(8,128)(2,1)S(1)} %copy-done, f32[32,2,6,384]{3,2,1,0:T(8,128)S(1)} %get-tuple-element.8, f32[32,2,6]{2,1,0:T(2,128)S(1)} %get-tuple-element.6, f32[32,2,6]{2,1,0:T(2,128)S(1)} %multiply_maximum_fusion, f32[32,2,128]{2,1,0:T(2,128)S(1)} %reshape.40, ...), kind=kOutput, calls=%fused_computation.3 | convolution fusion | flops 38338560 | bytes 7016960 | tf_op jit(solution)/shard_map/rkgp,rkpd->rkgd/dot_general | solution.py:43
  10.5 0.8 convert_element_type.31.att_ref
  11.2 68.3 %shard_map.136 = bf16[32,1536]{1,0:T(8,128)(2,1)} custom-call(bf16[32,1536]{1,0:T(8,128)(2,1)} %convert_element_type.31.att_ref, bf16[32,1536]{1,0:T(8,128)(2,1)} %resid_ref.1, f32[1536]{0:T(1024)} %gain_ref.1, s32[2,128]{1,0:T(2,128)} %bitcast.11, f32[2,128]{1,0:T(2,128)} %bitcast.12, bf16[1536,1536]{1,0:T(8,128)(2,1)} %wo_hbm.1, ...), custom_call_target="tpu_custom_call" | custom-call | flops 9663676416 | bytes 75497472 | tf_op jit(solution)/shard_map/pallas_call | solution.py:389
  79.6 1.5 %copy.18 = bf16[32,1536]{1,0:T(8,128)(2,1)} copy(bf16[32,1536]{1,0:T(8,128)(2,1)} %shard_map.136) | data formatting | bytes 196608
  (1 shorter events, 0.0 us)
Async XLA Ops:
  3.2 5.9 %copy-start = (bf16[32,2,384,128]{3,2,1,0:T(8,128)(2,1)S(1)}, bf16[32,2,384,128]{3,2,1,0:T(8,128)(2,1)}, u32[]{:S(2)}) copy-start(bf16[32,2,384,128]{3,2,1,0:T(8,128)(2,1)} %param.16) | copy-start | bytes 18874372

commit v4 on v3

--- a/solution.py
+++ b/solution.py
@@ -195,6 +195,10 @@
         p = npeer(d)
         remote(att_ref, att_all.at[rows(p)], att_s.at[d], att_r.at[p], p, t).wait_recv()
 
+    def proj_block(p, source, j):
+        cols = pl.ds(j * CHUNK, CHUNK)
+        return proj_send.at[rows(p), cols], proj_recv.at[source, :, cols]
+
     for j in range(F // CHUNK):
         wo_copy(j).wait()
         part = jnp.dot(
@@ -202,17 +206,16 @@
         )
         acc[:, j * CHUNK : (j + 1) * CHUNK] = part
         proj_send[:, j * CHUNK : (j + 1) * CHUNK] = part.astype(jnp.bfloat16)
-    for d in (2, 1, 3):
-        p = tpeer(d)
-        send(proj_send.at[rows(p)], proj_recv.at[t], pr_s.at[d], pr_r.at[t], n, p)
+        for d in (2, 1, 3):
+            p = tpeer(d)
+            send(*proj_block(p, t, j), pr_s.at[j, d], pr_r.at[j, t], n, p)
     for slot in range(wo_first, SLOTS):
         gu_copy(slot).start()
     total = resid_ref[...].astype(jnp.float32) + acc[rows(t), :]
     for d in range(1, T):
         p = tpeer(d)
-        remote(
-            proj_send.at[rows(p)], proj_recv.at[p], pr_s.at[d], pr_r.at[p], n, p
-        ).wait_recv()
+        for j in range(PARTS):
+            remote(*proj_block(p, p, j), pr_s.at[j, d], pr_r.at[j, p], n, p).wait_recv()
         total = total + proj_recv[p].astype(jnp.float32)
     hidden[...] = total
 
@@ -411,8 +414,8 @@
             dma((slots,)),
             dma((4,)),
             dma((4,)),
-            dma((tp,)),
-            dma((tp,)),
+            dma((F // CHUNK, tp)),
+            dma((F // CHUNK, tp)),
             dma((4,)),
             dma((4,)),
             dma((tp,)),

time: 81.4 us -> 80.9 us (level)
  no operation moved by 1% of the time
where the time goes in v4:
time: 80.9 us; the launch traced here: 80.6 us
  Pallas kernels  67.8 us (84%)
  matrix products  6.78 us (8%)
  local copies, waits for them, and re-layouts  4.82 us (6%)
  other arithmetic  1.12 us (1%)
    pallas_call x1, Pallas kernels, fused_layer(): pl.pallas_call(functools.partial(layer_kernel, tp), out_shape=jax.ShapeDt...  67.8 us
    dot_general x1, matrix products, attend_block(): jnp.einsum('rkgd,rkpd->rkgp', query_heads, cache_keys, preferred_element_...  5.32 us

profile of v4, /device:TPU:0, one launch (start us, length us, event | category | flops | bytes accessed | tf_op | source)
XLA Modules:
  0.0 80.6 jit_solution(16064433132892485029)
XLA Ops:
  0.0 0.7 iota_compare_fusion
  0.7 0.7 reshape.44
  1.5 0.7 reshape.40
  2.2 1.0 %reshape.38 = bf16[32,2,6,128]{3,2,1,0:T(8,128)(2,1)S(1)} reshape(bf16[32,1536]{1,0:T(8,128)(2,1)} %param.14) | data formatting | bytes 196608 | tf_op jit(solution)/shard_map/reshape | solution.py:25
  3.2 0.0 copy-start
  3.2 0.2 fusion.8
  3.4 5.3 %fusion.7 = (f32[32,2,6]{2,1,0:T(2,128)S(1)}, f32[32,2,6,384]{3,2,1,0:T(8,128)S(1)}) fusion(bf16[32,2,6,128]{3,2,1,0:T(8,128)(2,1)S(1)} %reshape.38, bf16[32,2,384,128]{3,2,1,0:T(8,128)(2,1)} %param.15, pred[32,384]{1,0:T(8,128)(4,1)S(1)} %iota_compare_fusion), kind=kOutput, calls=%fused_computation.15 | convolution fusion | flops 38190720 | bytes 6993408 | tf_op jit(solution)/shard_map/rkgd,rkpd->rkgp/dot_general | solution.py:27
  8.8 0.3 fusion.2
  9.1 0.1 fusion.5
  9.2 0.0 copy-done
  9.2 1.3 %fusion.1 = bf16[32,2,6,128]{3,2,1,0:T(8,128)(2,1)S(1)} fusion(bf16[32,2,384,128]{3,2,1,0:T(8,128)(2,1)S(1)} %copy-done, f32[32,2,6,384]{3,2,1,0:T(8,128)S(1)} %get-tuple-element.8, f32[32,2,6]{2,1,0:T(2,128)S(1)} %get-tuple-element.6, f32[32,2,6]{2,1,0:T(2,128)S(1)} %multiply_maximum_fusion, f32[32,2,128]{2,1,0:T(2,128)S(1)} %reshape.40, ...), kind=kOutput, calls=%fused_computation.3 | convolution fusion | flops 38338560 | bytes 7016960 | tf_op jit(solution)/shard_map/rkgp,rkpd->rkgd/dot_general | solution.py:43
  10.5 0.8 convert_element_type.31.att_ref
  11.2 67.8 %shard_map.136 = bf16[32,1536]{1,0:T(8,128)(2,1)} custom-call(bf16[32,1536]{1,0:T(8,128)(2,1)} %convert_element_type.31.att_ref, bf16[32,1536]{1,0:T(8,128)(2,1)} %resid_ref.1, f32[1536]{0:T(1024)} %gain_ref.1, s32[2,128]{1,0:T(2,128)} %bitcast.11, f32[2,128]{1,0:T(2,128)} %bitcast.12, bf16[1536,1536]{1,0:T(8,128)(2,1)} %wo_hbm.1, ...), custom_call_target="tpu_custom_call" | custom-call | flops 9663676416 | bytes 75497472 | tf_op jit(solution)/shard_map/pallas_call | solution.py:392
  79.0 1.5 %copy.18 = bf16[32,1536]{1,0:T(8,128)(2,1)} copy(bf16[32,1536]{1,0:T(8,128)(2,1)} %shard_map.136) | data formatting | bytes 196608
  (1 shorter events, 0.0 us)
Async XLA Ops:
  3.2 5.9 %copy-start = (bf16[32,2,384,128]{3,2,1,0:T(8,128)(2,1)S(1)}, bf16[32,2,384,128]{3,2,1,0:T(8,128)(2,1)}, u32[]{:S(2)}) copy-start(bf16[32,2,384,128]{3,2,1,0:T(8,128)(2,1)} %param.16) | copy-start | bytes 18874372
